TPU v7x, 32 devices: a whole 2x2x4 slice. The times are simulated.
32 devices in a mesh: dp: 4 (over y, x), expert: 4 (over z), tensor: 2 (over core).
Axes of the slice: x: 2, y: 2, z: 4, core: 2. Of those that a mesh axis runs over, the one named last changes fastest.
Arguments:
- tokens: bfloat16 [192, 3072], P('expert', 'tensor'), may hold values from -6 to 6
- cotangent: bfloat16 [192, 3072], P('expert', 'tensor'), may hold values from -6 to 6
- expert_ids: int32 [192, 2], P('expert'), may hold values from 0 to 3, all different within a row; in each aligned block of 48 rows (0 to 47, 48 to 95, ...) at most 32 rows name the same one
- gate_probs: bfloat16 [192, 2], P('expert'), may hold values from 0.049804688 to 0.94921875
- tenant_ids: int32 [192], P('expert'), may hold values from 0 to 7
- w_gate: bfloat16 [4, 3072, 1024], P('expert', None, ('dp', 'tensor')), may hold values from -0.109375 to 0.109375
- w_up: bfloat16 [4, 3072, 1024], P('expert', None, ('dp', 'tensor')), may hold values from -0.109375 to 0.109375
- w_down: bfloat16 [4, 1024, 3072], P('expert', ('dp', 'tensor')), may hold values from -0.1875 to 0.1875
- adapter_in: bfloat16 [4, 1024, 128], P('expert', ('dp', 'tensor')), may hold values from -0.1875 to 0.1875
- adapter_out: bfloat16 [4, 128, 3072], P('expert'), may hold values from -0.109375 to 0.109375
Outputs:
- input_grad: bfloat16 [192, 3072], P('expert', ('dp', 'tensor'))
- grad_in: float32 [4, 1024, 128], P('expert', ('dp', 'tensor'))
- grad_out: float32 [4, 128, 3072], P('expert', None, 'tensor')
Inputs may be any that keep to these rules, and one draw needn't show every extreme that they name: `expert_ids`: the two experts of a token differ. Among the 48 tokens of each group (aligned blocks of the token rows of one index of expert), no expert is named more than 32 times, and in every draw some expert is named exactly 32 times in some group.
All inputs are finite; a program needn't handle non-finite values.
Results may differ from a plain program's by a relative error of at most 0.005.
Values may be sent and summed in bfloat16 or wider, within the bound.
A program may use at most 64 MiB of HBM per device.

v0:
```python
import jax
import jax.numpy as jnp
from jax import lax
from jax.sharding import PartitionSpec as P

TEN = 8
RANK = 16
TOP = 2
CAP = 32


adapter_scale_factor = 2.0


def on_device(
    tokens,
    cotangent,
    expert_ids,
    gate_probs,
    tenant_ids,
    w_gate,
    w_up,
    w_down,
    adapter_in,
    adapter_out,
):
    experts = lax.axis_size("expert")
    tok_rows = tokens.shape[0]
    col_width = tokens.shape[1]
    slot_count = experts * CAP
    route_ids = expert_ids.reshape(-1)
    route_total = route_ids.shape[0]
    onehot = (route_ids[:, None] == jnp.arange(experts, dtype=jnp.int32)[None, :]).astype(jnp.int32)
    earlier = jnp.cumsum(onehot, axis=0) - onehot
    slot_index = jnp.sum(earlier * onehot, axis=1)
    target = route_ids * CAP + slot_index
    owner_token = jnp.arange(route_total, dtype=jnp.int32) // TOP
    slot_hits = (target[None, :] == jnp.arange(slot_count, dtype=jnp.int32)[:, None]).astype(
        jnp.float32
    )
    token_hits = (owner_token[:, None] == jnp.arange(tok_rows, dtype=jnp.int32)[None, :]).astype(
        jnp.float32
    )
    dispatch = jnp.dot(slot_hits, token_hits, precision=lax.Precision.HIGHEST)
    tenant_hot = (tenant_ids[:, None] == jnp.arange(TEN, dtype=jnp.int32)[None, :]).astype(
        jnp.float32
    )
    route_weight = gate_probs.reshape(-1).astype(jnp.float32)
    route_marks = (
        jnp.dot(token_hits, tenant_hot, precision=lax.Precision.HIGHEST) * route_weight[:, None]
    )
    slot_marks = jnp.dot(slot_hits, route_marks, precision=lax.Precision.HIGHEST)
    dispatch_half = dispatch.astype(jnp.bfloat16)
    send_inputs = jnp.dot(dispatch_half, tokens, preferred_element_type=jnp.float32).astype(
        jnp.bfloat16
    )
    send_grads = jnp.dot(dispatch_half, cotangent, preferred_element_type=jnp.float32).astype(
        jnp.bfloat16
    )
    send_inputs = send_inputs.reshape(experts, CAP, col_width)
    send_grads = send_grads.reshape(experts, CAP, col_width)
    send_marks = slot_marks.astype(jnp.bfloat16).reshape(experts, CAP, TEN)
    recv_inputs, recv_grads, recv_marks = (
        lax.all_to_all(send_inputs, "expert", split_axis=0, concat_axis=0, tiled=True),
        lax.all_to_all(send_grads, "expert", split_axis=0, concat_axis=0, tiled=True),
        lax.all_to_all(send_marks, "expert", split_axis=0, concat_axis=0, tiled=True),
    )
    gate_mat = w_gate[0]
    up_mat = w_up[0]
    down_mat = w_down[0]
    first_factor = adapter_in[0]
    second_factor = adapter_out[0]
    hidden_units = gate_mat.shape[1]
    low_width = first_factor.shape[1]
    input_piece = lax.all_gather(recv_inputs, "tensor", axis=2, tiled=True)
    grad_piece = lax.all_gather(recv_grads, "tensor", axis=2, tiled=True)
    piece_width = input_piece.shape[2]
    input_piece = input_piece.reshape(slot_count, piece_width)
    grad_piece = grad_piece.reshape(slot_count, piece_width)
    gate_rows = gate_mat
    up_projection_rows = up_mat
    gate_acc = jnp.dot(input_piece, gate_rows, preferred_element_type=jnp.float32)
    up_acc = jnp.dot(input_piece, up_projection_rows, preferred_element_type=jnp.float32)
    back_acc = lax.dot_general(
        grad_piece, down_mat, (((1,), (1,)), ((), ())), preferred_element_type=jnp.float32
    )
    low_acc = lax.dot_general(
        grad_piece, second_factor, (((1,), (1,)), ((), ())), preferred_element_type=jnp.float32
    )
    sig = jax.nn.sigmoid(gate_acc)
    silu_val = gate_acc * sig
    hidden = (silu_val * up_acc).astype(jnp.bfloat16)
    low_part = jnp.dot(hidden, first_factor, preferred_element_type=jnp.float32)
    marks_value = recv_marks.reshape(slot_count, TEN).astype(jnp.float32)
    row_weight = jnp.sum(marks_value, axis=1)
    broadcast_routing_flags = jnp.repeat(marks_value, RANK, axis=1)
    low_in = lax.psum(low_part, ("dp", "tensor"))
    gate_weighted_rows = adapter_scale_factor * broadcast_routing_flags
    down_coef = (gate_weighted_rows * low_acc).astype(jnp.bfloat16)
    up_coef = (gate_weighted_rows * low_in).astype(jnp.bfloat16)
    hidden_gradient = row_weight[:, None] * back_acc + lax.dot_general(
        down_coef, first_factor, (((1,), (1,)), ((), ())), preferred_element_type=jnp.float32
    )
    slope = sig * (1.0 + gate_acc * (1.0 - sig))
    gate_grad = (hidden_gradient * up_acc * slope).astype(jnp.bfloat16)
    up_grad = (hidden_gradient * silu_val).astype(jnp.bfloat16)
    grad_a = lax.dot_general(
        hidden, down_coef, (((0,), (0,)), ((), ())), preferred_element_type=jnp.float32
    )
    local_grads = recv_grads.reshape(slot_count, col_width)
    grad_b = lax.dot_general(
        up_coef, local_grads, (((0,), (0,)), ((), ())), preferred_element_type=jnp.float32
    )
    gate_rows = gate_mat
    up_projection_rows = up_mat
    term = lax.dot_general(
        gate_rows, gate_grad, (((1,), (1,)), ((), ())), preferred_element_type=jnp.float32
    )
    slices = lax.psum_scatter(
        term
        + lax.dot_general(
            up_projection_rows,
            up_grad,
            (((1,), (1,)), ((), ())),
            preferred_element_type=jnp.float32,
        ),
        ("dp", "tensor"),
        scatter_dimension=0,
        tiled=True,
    )
    slice_width = slices.shape[0]
    returned = lax.all_to_all(
        slices.reshape(slice_width, experts, CAP), "expert", split_axis=1, concat_axis=1, tiled=True
    )
    returned = returned.reshape(slice_width, slot_count)
    token_grad = lax.dot_general(
        dispatch,
        returned,
        (((0,), (1,)), ((), ())),
        precision=lax.Precision.HIGHEST,
        preferred_element_type=jnp.float32,
    )
    input_grad = token_grad.astype(jnp.bfloat16)
    return (
        input_grad,
        grad_a.reshape(1, hidden_units, low_width),
        grad_b.reshape(1, low_width, col_width),
    )


def solution(mesh):
    placed = (
        P("expert", "tensor"),
        P("expert", "tensor"),
        P("expert", None),
        P("expert", None),
        P("expert"),
        P("expert", None, ("dp", "tensor")),
        P("expert", None, ("dp", "tensor")),
        P("expert", ("dp", "tensor"), None),
        P("expert", ("dp", "tensor"), None),
        P("expert", None, None),
    )
    return jax.shard_map(
        on_device,
        mesh=mesh,
        in_specs=placed,
        out_specs=(
            P("expert", ("dp", "tensor")),
            P("expert", ("dp", "tensor"), None),
            P("expert", None, "tensor"),
        ),
        check_vma=False,
    )
```

profile of v0, /device:TPU:0, one launch (start us, length us, event | category | flops | bytes accessed | tf_op | source)
XLA Modules:
  0.0 165.6 jit_solution(10317815913440402445)
XLA Ops:
  7.2 0.0 copy-start
  7.2 0.0 copy-start.3
  7.2 0.9 copy.24
  8.0 0.1 reshape.80
  8.2 0.1 fusion.14
  8.3 0.1 reduce_window_sum.11
  8.4 0.2 select_reduce_fusion
  8.6 0.8 copy.25
  9.3 0.1 reshape.91
  9.5 0.9 convolution_multiply_fusion.2
  10.4 0.1 convolution_convert_fusion.3
  10.5 0.1 reshape.81
  10.6 0.7 reshape.92
  11.3 6.3 %all-to-all-start = ((bf16[4,2,128]{2,1,0:T(2,128)(2,1)}), bf16[4,2,128]{2,1,0:T(2,128)(2,1)S(1)}, u32[]{:S(2)}, u32[]{:S(2)}) async-start(bf16[4,2,128]{2,1,0:T(2,128)(2,1)} %reshape.92), calls=%async_computation | async-start | bytes 4096 | tf_op jit(solution)/shard_map/all_to_all | solution.py:66
  17.6 0.3 fusion.13
  17.9 1.9 %convolution_convert_fusion.1 = bf16[128,1536]{1,0:T(8,128)(2,1)} fusion(bf16[48,1536]{1,0:T(8,128)(2,1)} %param.11, f32[128,48]{0,1:T(8,128)S(1)} %fusion.13), kind=kOutput, calls=%fused_computation.4 | convolution fusion | flops 19077120 | bytes 565248 | tf_op jit(solution)/shard_map/dot_general | solution.py:57
  19.8 3.3 %all-to-all-done = bf16[4,2,128]{2,1,0:T(2,128)(2,1)S(1)} async-done(((bf16[4,2,128]{2,1,0:T(2,128)(2,1)}), bf16[4,2,128]{2,1,0:T(2,128)(2,1)S(1)}, u32[]{:S(2)}, u32[]{:S(2)}) %all-to-all-start) | async-done | bytes 2080 | tf_op jit(solution)/shard_map/all_to_all | solution.py:66
  23.1 3.5 %all-to-all-start.1 = ((bf16[4,32,1536]{2,1,0:T(8,128)(2,1)}), bf16[4,32,1536]{2,1,0:T(8,128)(2,1)S(1)}, u32[]{:S(2)}, u32[]{:S(2)}) async-start(bf16[4,32,1536]{2,1,0:T(8,128)(2,1)} %bitcast), calls=%async_computation.1 | async-start | bytes 786432 | tf_op jit(solution)/shard_map/all_to_all | solution.py:65
  26.6 0.0 copy-done.3
  26.6 1.0 convolution_convert_fusion
  27.6 0.1 reshape.93
  27.7 0.1 mul.81
  27.8 0.1 copy.28
  27.9 0.1 mul.76
  28.0 9.1 %all-to-all-done.1 = bf16[4,32,1536]{2,1,0:T(8,128)(2,1)S(1)} async-done(((bf16[4,32,1536]{2,1,0:T(8,128)(2,1)}), bf16[4,32,1536]{2,1,0:T(8,128)(2,1)S(1)}, u32[]{:S(2)}, u32[]{:S(2)}) %all-to-all-start.1) | async-done | bytes 393248 | tf_op jit(solution)/shard_map/all_to_all | solution.py:65
  37.1 3.5 %all-to-all-start.2 = ((bf16[4,32,1536]{2,1,0:T(8,128)(2,1)}), bf16[4,32,1536]{2,1,0:T(8,128)(2,1)S(1)}, u32[]{:S(2)}, u32[]{:S(2)}) async-start(bf16[4,32,1536]{2,1,0:T(8,128)(2,1)} %bitcast.6), calls=%async_computation.2 | async-start | bytes 786432 | tf_op jit(solution)/shard_map/all_to_all | solution.py:64
  40.5 0.0 copy-start.4
  40.6 0.0 reduce-scatter.2.cloned.1.call-start
  40.6 2.4 %all_gather.6 = bf16[4,32,3072]{2,1,0:T(8,128)(2,1)S(1)} all-gather(bf16[4,32,1536]{2,1,0:T(8,128)(2,1)S(1)} %all-to-all-done.1), channel_id=1, replica_groups=mesh['dp'=4,'expert'=4,'tensor'=2] {'tensor'}, dimensions={2}, use_global_device_ids=true | all-gather | bytes 1179648 | tf_op jit(solution)/shard_map/all_gather | solution.py:76
  43.0 0.0 copy-start.1
  43.0 1.6 fusion.2
  44.6 0.0 copy-done.4
  44.6 0.1 fusion.17
  44.7 5.6 %all-to-all-done.2 = bf16[4,32,1536]{2,1,0:T(8,128)(2,1)S(1)} async-done(((bf16[4,32,1536]{2,1,0:T(8,128)(2,1)}), bf16[4,32,1536]{2,1,0:T(8,128)(2,1)S(1)}, u32[]{:S(2)}, u32[]{:S(2)}) %all-to-all-start.2) | async-done | bytes 393248 | tf_op jit(solution)/shard_map/all_to_all | solution.py:64
  50.3 2.4 %all_gather.7 = bf16[4,32,3072]{2,1,0:T(8,128)(2,1)S(1)} all-gather(bf16[4,32,1536]{2,1,0:T(8,128)(2,1)S(1)} %all-to-all-done.2), channel_id=1, replica_groups=mesh['dp'=4,'expert'=4,'tensor'=2] {'tensor'}, dimensions={2}, use_global_device_ids=true | all-gather | bytes 1179648 | tf_op jit(solution)/shard_map/all_gather | solution.py:75
  52.7 0.0 copy-done.1
  52.7 0.0 copy-start.2
  52.7 0.4 fusion.5
  53.1 0.0 copy-done
  53.1 0.4 multiply_convert_fusion.1
  53.5 0.4 copy-done.2
  53.8 0.4 fusion.1
  54.2 0.4 fusion.3
  54.6 1.5 fusion
  56.1 0.0 reduce-scatter.2.cloned.1.call-update
  56.1 37.7 %reduce-scatter.2.cloned.1.call-done = f32[384,128]{0,1:T(8,128)} async-done(((f32[3072,128]{0,1:T(8,128)}), f32[384,128]{0,1:T(8,128)}) %reduce-scatter.2.cloned.1.call-update) | async-done | bytes 196624 | tf_op jit(solution)/shard_map/reduce_scatter | solution.py:119
  93.9 4.6 %all-to-all-start.3 = ((f32[384,4,32]{0,2,1:T(8,128)}), f32[384,4,32]{0,2,1:T(8,128)S(1)}, u32[]{:S(2)}, u32[]{:S(2)}) async-start(f32[384,4,32]{0,2,1:T(8,128)} %bitcast.67), calls=%async_computation.4 | async-start | bytes 393216 | tf_op jit(solution)/shard_map/all_to_all | solution.py:132
  98.5 0.0 all-reduce.2.cloned.1.call-start
  98.5 0.8 fusion.15
  99.2 0.0 all-reduce.2.cloned.1.call-update
  99.3 0.8 convolution_bitcast_fusion.1
  100.1 55.8 %all-reduce.2.cloned.1.call-done = f32[128,128]{1,0:T(8,128)} async-done(((f32[128,128]{1,0:T(8,128)}), f32[128,128]{1,0:T(8,128)}) %all-reduce.2.cloned.1.call-update) | async-done | bytes 65552 | tf_op jit(solution)/shard_map/psum | solution.py:97
  155.9 2.0 %convolution_bitcast_fusion = f32[1,128,1536]{2,1,0:T(8,128)} fusion(bf16[128,1536]{1,0:T(8,128)(2,1)S(1)} %bitcast.64, f32[128,128]{1,0:T(8,128)S(1)} %copy.28, f32[128,128]{1,0:T(8,128)} %all-reduce.2.cloned.1.call-done), kind=kOutput, calls=%fused_computation.2 | convolution fusion | flops 50364416 | bytes 1310720 | tf_op jit(solution)/shard_map/dot_general | solution.py:111
  157.9 0.0 all-to-all-done.3
  157.9 0.9 convolution_convert_fusion.2
  (5 shorter events, 0.0 us)
Async XLA Ops:
  7.2 45.9 %copy-start = (bf16[1,3072,128]{2,1,0:T(8,128)(2,1)S(1)}, bf16[1,3072,128]{2,1,0:T(8,128)(2,1)}, u32[]{:S(2)}) copy-start(bf16[1,3072,128]{2,1,0:T(8,128)(2,1)} %param.16) | copy-start | bytes 2359300
  7.2 19.4 %copy-start.3 = (bf16[48,1536]{1,0:T(8,128)(2,1)S(1)}, bf16[48,1536]{1,0:T(8,128)(2,1)}, u32[]{:S(2)}) copy-start(bf16[48,1536]{1,0:T(8,128)(2,1)} %param.10) | copy-start | bytes 442372
  11.3 11.8 %all-to-all-start = ((bf16[4,2,128]{2,1,0:T(2,128)(2,1)}), bf16[4,2,128]{2,1,0:T(2,128)(2,1)S(1)}, u32[]{:S(2)}, u32[]{:S(2)}) async-start(bf16[4,2,128]{2,1,0:T(2,128)(2,1)} %reshape.92), calls=%async_computation | async-start | bytes 4096 | tf_op jit(solution)/shard_map/all_to_all | solution.py:66
  23.1 14.0 %all-to-all-start.1 = ((bf16[4,32,1536]{2,1,0:T(8,128)(2,1)}), bf16[4,32,1536]{2,1,0:T(8,128)(2,1)S(1)}, u32[]{:S(2)}, u32[]{:S(2)}) async-start(bf16[4,32,1536]{2,1,0:T(8,128)(2,1)} %bitcast), calls=%async_computation.1 | async-start | bytes 786432 | tf_op jit(solution)/shard_map/all_to_all | solution.py:65
  37.1 13.3 %all-to-all-start.2 = ((bf16[4,32,1536]{2,1,0:T(8,128)(2,1)}), bf16[4,32,1536]{2,1,0:T(8,128)(2,1)S(1)}, u32[]{:S(2)}, u32[]{:S(2)}) async-start(bf16[4,32,1536]{2,1,0:T(8,128)(2,1)} %bitcast.6), calls=%async_computation.2 | async-start | bytes 786432 | tf_op jit(solution)/shard_map/all_to_all | solution.py:64
  40.5 4.0 %copy-start.4 = (bf16[1,128,128]{2,1,0:T(8,128)(2,1)S(1)}, bf16[1,128,128]{2,1,0:T(8,128)(2,1)}, u32[]{:S(2)}) copy-start(bf16[1,128,128]{2,1,0:T(8,128)(2,1)} %param.18) | copy-start | bytes 98308
  40.6 53.3 %reduce-scatter.2.cloned.1.call-start = ((), (), s32[]{:S(2)}) async-start(), calls=%async_computation.5 | async-start | bytes 1769472 | tf_op jit(solution)/shard_map/reduce_scatter | solution.py:119
  43.0 9.7 %copy-start.1 = (bf16[1,3072,128]{2,1,0:T(8,128)(2,1)S(1)}, bf16[1,3072,128]{2,1,0:T(8,128)(2,1)}, u32[]{:S(2)}) copy-start(bf16[1,3072,128]{2,1,0:T(8,128)(2,1)} %param.15) | copy-start | bytes 2359300
  52.7 1.1 copy-start.2
  93.9 64.0 %all-to-all-start.3 = ((f32[384,4,32]{0,2,1:T(8,128)}), f32[384,4,32]{0,2,1:T(8,128)S(1)}, u32[]{:S(2)}, u32[]{:S(2)}) async-start(f32[384,4,32]{0,2,1:T(8,128)} %bitcast.67), calls=%async_computation.4 | async-start | bytes 393216 | tf_op jit(solution)/shard_map/all_to_all | solution.py:132
  98.5 57.4 %all-reduce.2.cloned.1.call-start = ((), (), s32[]{:S(2)}) async-start(), calls=%async_computation.6 | async-start | bytes 131072 | tf_op jit(solution)/shard_map/psum | solution.py:97
Sparse Core Ops, SparseCore 0:
  56.2 37.5 reduce-scatter.1
  102.9 52.9 all-reduce.1
where the time goes:
time: 166 us
  waiting for transfers between devices  112 us (67%)
  starting transfers between devices  17.9 us (11%)
  between operations  14.2 us (9%)
  matrix products  13.4 us (8%)
  blocking collectives  4.73 us (3%)
  local copies, waits for them, and re-layouts  3.41 us (2%)
    psum x1, waiting for transfers between devices, on_device(): low_in = lax.psum(low_part, ('dp', 'tensor'))  55.8 us
    reduce_scatter x1, waiting for transfers between devices, on_device(): lax.psum_scatter(term + lax.dot_general(up_projection_rows, up_grad, (((1...  37.7 us
    all_to_all x1, waiting for transfers between devices, on_device(): lax.all_to_all(send_grads, 'expert', split_axis=0, concat_axis=0, tiled=T...  9.07 us
    all_to_all x1, starting transfers between devices, on_device(): lax.all_to_all(send_marks, 'expert', split_axis=0, concat_axis=0, tiled=T...  6.32 us
    all_to_all x1, waiting for transfers between devices, on_device(): lax.all_to_all(send_inputs, 'expert', split_axis=0, concat_axis=0, tiled=...  5.63 us
    all_to_all x1, starting transfers between devices, on_device(): lax.all_to_all(slices.reshape(slice_width, experts, CAP), 'expert', split...  4.6 us
    all_to_all x1, starting transfers between devices, on_device(): lax.all_to_all(send_inputs, 'expert', split_axis=0, concat_axis=0, tiled=...  3.46 us
    all_to_all x1, starting transfers between devices, on_device(): lax.all_to_all(send_grads, 'expert', split_axis=0, concat_axis=0, tiled=T...  3.46 us
  transfers between devices with their start and end apart: 6, of which 5 were waited for; matrix products, arithmetic and copies ran while one was open for 5% of the time, Pallas kernels for 0%

commit v1 on v0

--- a/solution.py
+++ b/solution.py
@@ -1,6 +1,10 @@
+import functools
+
 import jax
 import jax.numpy as jnp
 from jax import lax
+from jax.experimental import pallas as pl
+from jax.experimental.pallas import tpu as pltpu
 from jax.sharding import PartitionSpec as P
 
 TEN = 8
@@ -148,6 +152,324 @@
     )
 
 
+MESH = pl.DeviceIdType.MESH
+LANES = 128
+F32 = jnp.float32
+BF16 = jnp.bfloat16
+
+
+def partner(index, step):
+    bit = 1
+    while bit <= step:
+        if step & bit:
+            index = index + bit - 2 * bit * lax.rem(lax.div(index, bit), 2)
+        bit *= 2
+    return index
+
+
+def tdot(a, b):
+    return lax.dot_general(a, b, (((0,), (0,)), ((), ())), preferred_element_type=F32)
+
+
+def ndot(a, b):
+    return lax.dot_general(a, b, (((1,), (1,)), ((), ())), preferred_element_type=F32)
+
+
+def layer_kernel(
+    sizes,
+    tok_ref, cot_ref, ids_ref, prob_ref, ten_ref, wg_ref, wu_ref, wd_ref, ain_ref, aout_ref,
+    dx_ref, ga_ref, gb_ref,
+    rows, send, wgu, wgb, wda, ain, mine, theirs, hid, grads, out_part, in_part, back_send, back, kept, low_mine, low_theirs,
+    local_sem, w_send, w_recv, z_send, z_recv, p_send, p_recv, s_send, s_recv,
+    r_send, r_recv, b_send, b_recv, l_send, l_recv,
+):
+    dp, ex, tn = sizes
+    d, e, t = lax.axis_index("dp"), lax.axis_index("expert"), lax.axis_index("tensor")
+    tokg, half = tok_ref.shape
+    wide = half // dp
+    ff = wg_ref.shape[3]
+    low = ain_ref.shape[2]
+    hall = tn * ff
+    slots = ex * CAP
+
+    barrier = pltpu.get_barrier_semaphore()
+    for axis, index, count in (("tensor", t, tn), ("dp", d, dp), ("expert", e, ex)):
+        for step in range(1, count):
+            pl.semaphore_signal(
+                barrier, inc=1, device_id={axis: partner(index, step)}, device_id_type=MESH
+            )
+
+    def remote(src, dst, ssem, rsem, axis, to):
+        return pltpu.make_async_remote_copy(
+            src_ref=src, dst_ref=dst, send_sem=ssem, recv_sem=rsem,
+            device_id={axis: to}, device_id_type=MESH,
+        )
+
+    def lanes(start, size):
+        return pl.ds(pl.multiple_of(start, LANES), size)
+
+    def weight_parts(feat_owner, hid_owner):
+        f = lanes(feat_owner * half, half)
+        run = pl.ds(feat_owner * (dp // tn), dp // tn)
+        gate_cols, up_cols = lanes(hid_owner * ff, ff), lanes(hall + hid_owner * ff, ff)
+        return (
+            (wg_ref.at[run], wgu.at[:, :, :, gate_cols]),
+            (wu_ref.at[run], wgu.at[:, :, :, up_cols]),
+            (wd_ref.at[0, :, f], wda.at[lanes(hid_owner * ff, ff), :]),
+            (ain_ref.at[0], ain.at[lanes(hid_owner * ff, ff), :]),
+            (wg_ref.at[:, feat_owner], wgb.at[:, :, gate_cols]),
+            (wu_ref.at[:, feat_owner], wgb.at[:, :, up_cols]),
+        )
+
+    local = [
+        pltpu.make_async_copy(s, o, local_sem.at[i])
+        for i, (s, o) in enumerate(weight_parts(t, t))
+    ]
+    local.append(
+        pltpu.make_async_copy(aout_ref.at[0, :, lanes(t * half, half)], wda.at[pl.ds(hall, low), :], local_sem.at[len(local)])
+    )
+    for c in local:
+        c.start()
+
+    ti = lax.broadcasted_iota(jnp.int32, (tokg, tokg), 0)
+    tj = lax.broadcasted_iota(jnp.int32, (tokg, tokg), 1)
+
+    def column(row):
+        wide_row = jnp.broadcast_to(row.astype(F32), (tokg, tokg))
+        return jnp.sum(jnp.where(ti == tj, wide_row, 0.0), axis=1, keepdims=True)
+
+    ids0, ids1 = column(ids_ref[0:1, :]).astype(jnp.int32), column(ids_ref[1:2, :]).astype(jnp.int32)
+    probs = prob_ref[...].astype(F32)
+    prob0, prob1 = column(probs[0:1, :]), column(probs[1:2, :])
+    col = lax.broadcasted_iota(jnp.int32, (tokg, slots), 1)
+    ecol = lax.div(col, CAP)
+    scol = col - ecol * CAP
+    hit0, hit1 = ids0 == ecol, ids1 == ecol
+    named = jnp.where(hit0 | hit1, 1.0, 0.0)
+    before = jnp.where(ti > tj, 1.0, 0.0).astype(BF16)
+    place = jnp.dot(before, named.astype(BF16), preferred_element_type=F32)
+    disp = jnp.where(place == scol.astype(F32), named, 0.0)
+    weight = jnp.where(hit0, prob0, 0.0) + jnp.where(hit1, prob1, 0.0)
+    tcol = column(ten_ref[...])
+    lowcol = lax.div(lax.broadcasted_iota(jnp.int32, (tokg, low), 1), RANK).astype(F32)
+    tmark = jnp.where(tcol == lowcol, 1.0, 0.0).astype(BF16)
+    marks = tdot((disp * weight).astype(BF16), tmark).astype(BF16)
+    disp = disp.astype(BF16)
+    mycols = lanes(d * wide, wide)
+    sx = tdot(disp, tok_ref[:, mycols]).astype(BF16)
+    sy = tdot(disp, cot_ref[:, mycols]).astype(BF16)
+    send[:, :, 0:wide] = sx.reshape(ex, CAP, wide)
+    send[:, :, wide:2 * wide] = sy.reshape(ex, CAP, wide)
+    send[:, :, 2 * wide:] = marks.reshape(ex, CAP, low)
+
+    pl.semaphore_wait(barrier, (tn - 1) + (dp - 1) + (ex - 1))
+
+    sends = []
+    for step in range(1, ex):
+        to = partner(e, step)
+        c = remote(send.at[to], rows.at[e, d], z_send.at[step], z_recv.at[e], "expert", to)
+        c.start()
+        sends.append(c)
+    for step in range(1, tn):
+        to = partner(t, step)
+        for i, (s, o) in enumerate(weight_parts(to, t)):
+            c = remote(s, o, w_send.at[step, i], w_recv.at[t, i], "tensor", to)
+            c.start()
+            sends.append(c)
+
+    scol_own = lax.broadcasted_iota(jnp.int32, (tokg, CAP), 1).astype(F32)
+    named_own = jnp.where((ids0 == e) | (ids1 == e), 1.0, 0.0)
+    named_own = jnp.broadcast_to(named_own, (tokg, CAP))
+    place_own = jnp.dot(before, named_own.astype(BF16), preferred_element_type=F32)
+    disp_own = jnp.where(place_own == scol_own, named_own, 0.0).astype(BF16)
+    for k in range(dp):
+        cols = slice(k * wide, (k + 1) * wide)
+        rows[e, k, :, 0:wide] = tdot(disp_own, tok_ref[:, cols]).astype(BF16)
+        rows[e, k, :, wide:2 * wide] = tdot(disp_own, cot_ref[:, cols]).astype(BF16)
+    rows[e, d, :, 2 * wide:] = send[e, :, 2 * wide:]
+
+    for step in range(1, ex):
+        g = partner(e, step)
+        remote(send.at[g], rows.at[g, d], z_send.at[step], z_recv.at[g], "expert", g).wait_recv()
+        for hop in range(1, dp):
+            to = partner(d, hop)
+            part = rows.at[g, d, :, pl.ds(0, 2 * wide)]
+            c = remote(part, part, p_send.at[step, hop], p_recv.at[g, d], "dp", to)
+            c.start()
+            sends.append(c)
+
+    for c in local:
+        c.wait()
+    for step in range(1, tn):
+        frm = partner(t, step)
+        for i, (s, o) in enumerate(weight_parts(t, frm)):
+            remote(s, o, w_send.at[step, i], w_recv.at[frm, i], "tensor", frm).wait_recv()
+
+    def products(g):
+        gu = jnp.zeros((CAP, 2 * hall), F32)
+        bl = jnp.zeros((CAP, hall + low), F32)
+        for k in range(dp):
+            f = slice(k * wide, (k + 1) * wide)
+            gu = gu + jnp.dot(rows[g, k, :, 0:wide], wgu[k // tn, k % tn], preferred_element_type=F32)
+            bl = bl + ndot(rows[g, k, :, wide:2 * wide], wda[:, f])
+        mine[g, :, 0:2 * hall] = gu
+        mine[g, :, 2 * hall:] = bl
+        for hop in range(1, tn):
+            to = partner(t, hop)
+            c = remote(mine.at[g], theirs.at[t, g], s_send.at[hop, step], s_recv.at[t, g], "tensor", to)
+            c.start()
+            sends.append(c)
+
+    for step in range(ex):
+        g = partner(e, step)
+        if step:
+            for hop in range(1, dp):
+                frm = partner(d, hop)
+                part = rows.at[g, frm, :, pl.ds(0, 2 * wide)]
+                remote(part, part, p_send.at[step, hop], p_recv.at[g, frm], "dp", frm).wait_recv()
+        products(g)
+
+    for step in range(ex):
+        g = partner(e, step)
+        for hop in range(1, tn):
+            frm = partner(t, hop)
+            remote(mine.at[g], theirs.at[frm, g], s_send.at[hop, step], s_recv.at[frm, g], "tensor", frm).wait_recv()
+    total = mine[...].reshape(slots, -1)
+    for hop in range(1, tn):
+        total = total + theirs[partner(t, hop)].reshape(slots, -1)
+    gate, up = total[:, 0:hall], total[:, hall:2 * hall]
+    back_acc, low_acc = total[:, 2 * hall:3 * hall], total[:, 3 * hall:]
+    flags = rows[:, d, :, 2 * wide:].reshape(slots, low).astype(F32)
+    row_weight = jnp.max(flags, axis=1, keepdims=True)
+    flags = adapter_scale_factor * flags
+    sig = jax.nn.sigmoid(gate)
+    silu = gate * sig
+    hidden = (silu * up).astype(BF16)
+    hid[...] = hidden
+    down_coef = (flags * low_acc).astype(BF16)
+    a_in = ain[...]
+    hidden_grad = row_weight * back_acc + ndot(down_coef, a_in)
+    slope = sig * (1.0 + gate * (1.0 - sig))
+    grads[:, 0:hall] = (hidden_grad * up * slope).astype(BF16)
+    grads[:, hall:] = (hidden_grad * silu).astype(BF16)
+
+    def slice_grad(k):
+        return ndot(grads[...], wgb[k])
+
+    for hop in range(dp - 1, 0, -1):
+        to = partner(d, hop)
+        out_part[hop] = slice_grad(to).astype(BF16).reshape(ex, CAP, wide)
+        for step in range(ex - 1, -1, -1):
+            g = partner(e, step)
+            c = remote(out_part.at[hop, g], in_part.at[d, g], r_send.at[hop, step], r_recv.at[d, g], "dp", to)
+            c.start()
+            sends.append(c)
+    own = slice_grad(d).reshape(ex, CAP, wide)
+    low_mine[...] = jnp.dot(hidden, a_in, preferred_element_type=F32)
+    for hop in range(1, dp):
+        c = remote(low_mine, low_theirs.at[d], l_send.at[hop], l_recv.at[d], "dp", partner(d, hop))
+        c.start()
+        sends.append(c)
+    kept[...] = own
+    ga_ref[0] = tdot(hid[:, lanes(t * ff, ff)], down_coef)
+
+    for step in range(ex - 1, -1, -1):
+        g = partner(e, step)
+        acc = kept[g]
+        for hop in range(dp - 1, 0, -1):
+            frm = partner(d, hop)
+            remote(out_part.at[hop, g], in_part.at[frm, g], r_send.at[hop, step], r_recv.at[frm, g], "dp", frm).wait_recv()
+            acc = acc + in_part[frm, g].astype(F32)
+        if step:
+            back_send[step] = acc.astype(BF16)
+            c = remote(back_send.at[step], back.at[e], b_send.at[step], b_recv.at[e], "expert", g)
+            c.start()
+            sends.append(c)
+        else:
+            back[e] = acc.astype(BF16)
+
+    low_in = low_mine[...]
+    for hop in range(1, dp):
+        frm = partner(d, hop)
+        remote(low_mine, low_theirs.at[frm], l_send.at[hop], l_recv.at[frm], "dp", frm).wait_recv()
+    low_in = low_in + sum(low_theirs[partner(d, hop)] for hop in range(1, dp))
+    up_coef = (flags * low_in).astype(BF16)
+    for k in range(dp):
+        y = rows[:, k, :, wide:2 * wide].reshape(slots, wide)
+        gb_ref[0, :, k * wide:(k + 1) * wide] = tdot(up_coef, y)
+
+    for step in range(1, ex):
+        g = partner(e, step)
+        remote(back_send.at[step], back.at[g], b_send.at[step], b_recv.at[g], "expert", g).wait_recv()
+    dx_ref[...] = jnp.dot(disp, back[...].reshape(slots, wide), preferred_element_type=F32).astype(BF16)
+    for c in sends:
+        c.wait_send()
+
+
+def fused(sizes, tokens, cotangent, expert_ids, gate_probs, tenant_ids, w_gate, w_up, w_down, adapter_in, adapter_out):
+    dp, ex, tn = sizes
+    tokg, half = tokens.shape
+    wide = half // dp
+    ff = w_gate.shape[2]
+    low = adapter_in.shape[2]
+    hall, slots = tn * ff, ex * CAP
+    vmem, hbm = pl.BlockSpec(memory_space=pltpu.VMEM), pl.BlockSpec(memory_space=pl.ANY)
+    dma = pltpu.SemaphoreType.DMA
+    return pl.pallas_call(
+        functools.partial(layer_kernel, sizes),
+        out_shape=(
+            jax.ShapeDtypeStruct((tokg, wide), BF16),
+            jax.ShapeDtypeStruct((1, ff, low), F32),
+            jax.ShapeDtypeStruct((1, low, half), F32),
+        ),
+        in_specs=[vmem] * 5 + [hbm] * 5,
+        out_specs=(vmem, vmem, vmem),
+        scratch_shapes=[
+            pltpu.VMEM((ex, dp, CAP, 2 * wide + low), BF16),
+            pltpu.VMEM((ex, CAP, 2 * wide + low), BF16),
+            pltpu.VMEM((dp // tn, tn, wide, 2 * hall), BF16),
+            pltpu.VMEM((dp, wide, 2 * hall), BF16),
+            pltpu.VMEM((hall + low, half), BF16),
+            pltpu.VMEM((hall, low), BF16),
+            pltpu.VMEM((ex, CAP, 3 * hall + low), F32),
+            pltpu.VMEM((tn, ex, CAP, 3 * hall + low), F32),
+            pltpu.VMEM((slots, hall), BF16),
+            pltpu.VMEM((slots, 2 * hall), BF16),
+            pltpu.VMEM((dp, ex, CAP, wide), BF16),
+            pltpu.VMEM((dp, ex, CAP, wide), BF16),
+            pltpu.VMEM((ex, CAP, wide), BF16),
+            pltpu.VMEM((ex, CAP, wide), BF16),
+            pltpu.VMEM((ex, CAP, wide), F32),
+            pltpu.VMEM((slots, low), F32),
+            pltpu.VMEM((dp, slots, low), F32),
+            dma((7,)),
+            dma((tn, 6)), dma((tn, 6)),
+            dma((ex,)), dma((ex,)),
+            dma((ex, dp)), dma((ex, dp)),
+            dma((tn, ex)), dma((tn, ex)),
+            dma((dp, ex)), dma((dp, ex)),
+            dma((ex,)), dma((ex,)),
+            dma((dp,)), dma((dp,)),
+        ],
+        compiler_params=pltpu.CompilerParams(
+            collective_id=0, has_side_effects=True, vmem_limit_bytes=40 * 1024 * 1024
+        ),
+        cost_estimate=pl.CostEstimate(flops=10**9, bytes_accessed=8 * 10**6, transcendentals=10**5),
+    )(tokens, cotangent, expert_ids.T, gate_probs.T, tenant_ids.reshape(1, -1), w_gate.reshape(dp, tn, wide, ff), w_up.reshape(dp, tn, wide, ff), w_down, adapter_in, adapter_out)
+
+
+def body_for(mesh):
+    sizes = (mesh.shape["dp"], mesh.shape["expert"], mesh.shape["tensor"])
+    paired = all(n & (n - 1) == 0 for n in sizes)
+
+    def body(tokens, *rest):
+        if paired and sizes[0] % sizes[2] == 0 and tokens.shape[1] % (sizes[0] * LANES) == 0:
+            return fused(sizes, tokens, *rest)
+        return on_device(tokens, *rest)
+
+    return body
+
+
 def solution(mesh):
     placed = (
         P("expert", "tensor"),
@@ -162,7 +484,7 @@
         P("expert", None, None),
     )
     return jax.shard_map(
-        on_device,
+        body_for(mesh),
         mesh=mesh,
         in_specs=placed,
         out_specs=(

time: 166 us -> 39.6 us (0.24)
  waiting for transfers between devices: 112 us -> 0 us
  Pallas kernels: 0 us -> 28.6 us
  starting transfers between devices: 17.9 us -> 0 us
  between operations: 14.2 us -> 0.68 us
  matrix products: 13.4 us -> 0 us
  local copies, waits for them, and re-layouts: 3.41 us -> 9.91 us
  blocking collectives: 4.73 us -> 0 us
    psum x1 -> x0, waiting for transfers between devices: 55.8 us -> none  [on_device(): low_in = lax.psum(low_part, ('dp', 'tensor'))]
    reduce_scatter x1 -> x0, waiting for transfers between devices: 37.7 us -> none  [on_device(): lax.psum_scatter(term + lax.dot_general(up_projection_rows, up_grad, (((1...]
    pallas_call x0 -> x1, Pallas kernels: none -> 28.6 us  [fused(): pl.pallas_call(functools.partial(layer_kernel, sizes), out_shape=(jax.Sha...]
    all_to_all x4 -> x0, waiting for transfers between devices: 18 us -> none  [the longest x1 9.07 us: on_device(): lax.all_to_all(send_grads, 'expert', split_axis=0, concat_axis=0, tiled=T...]
    all_to_all x4 -> x0, starting transfers between devices: 17.8 us -> none  [the longest x1 6.32 us: on_device(): lax.all_to_all(send_marks, 'expert', split_axis=0, concat_axis=0, tiled=T...]
    dot_general x16 -> x0, matrix products: 13.4 us -> none  [the longest x1 2.02 us: on_device(): lax.dot_general(up_coef, local_grads, (((0,), (0,)), ((), ())), preferred...]
    unnamed x13 -> x23, local copies, waits for them, and re-layouts: 2.07 us -> 9.91 us
    all_gather x2 -> x0, blocking collectives: 4.73 us -> none  [the longest x1 2.37 us: on_device(): grad_piece = lax.all_gather(recv_grads, 'tensor', axis=2, tiled=True)]
  transfers between devices with their start and end apart: 6 -> 0, of which waited for: 5 -> 0; matrix products, arithmetic and copies ran while one was open for 5% -> 0% of each run, Pallas kernels for 0% -> 0%
where the time goes in v1:
time: 39.6 us; the launch traced here: 39.1 us
  Pallas kernels  28.6 us (72%)
  local copies, waits for them, and re-layouts  9.91 us (25%)
  between operations  0.68 us (2%)
    pallas_call x1, Pallas kernels, fused(): pl.pallas_call(functools.partial(layer_kernel, sizes), out_shape=(jax.Sha...  28.6 us
    unnamed x23, local copies, waits for them, and re-layouts  9.91 us

profile of v1, /device:TPU:0, one launch (start us, length us, event | category | flops | bytes accessed | tf_op | source)
XLA Modules:
  0.0 39.1 jit_solution(8311482909877804236)
XLA Ops:
  0.6 0.0 copy-start.9
  0.6 0.0 copy-start.7
  0.7 0.0 copy-start.8
  0.7 0.6 %copy-done.9 = s32[48]{0:T(128)S(1)} copy-done((s32[48]{0:T(128)S(1)}, s32[48]{0:T(128)}, u32[]{:S(2)}) %copy-start.9) | copy-done | bytes 216
  1.3 0.0 copy-done.7
  1.3 0.0 copy-done.8
  1.3 0.0 copy-start
  1.3 1.1 %copy-done = bf16[1,3072,128]{2,1,0:T(8,128)(2,1)S(1)} copy-done((bf16[1,3072,128]{2,1,0:T(8,128)(2,1)S(1)}, bf16[1,3072,128]{2,1,0:T(8,128)(2,1)}, u32[]{:S(2)}) %copy-start) | copy-done | bytes 786456
  2.5 0.0 copy-start.1
  2.5 1.1 %copy-done.1 = bf16[1,3072,128]{2,1,0:T(8,128)(2,1)S(1)} copy-done((bf16[1,3072,128]{2,1,0:T(8,128)(2,1)S(1)}, bf16[1,3072,128]{2,1,0:T(8,128)(2,1)}, u32[]{:S(2)}) %copy-start.1) | copy-done | bytes 786456
  3.6 0.0 copy-start.2
  3.6 1.1 %copy-done.2 = bf16[1,128,3072]{2,1,0:T(8,128)(2,1)S(1)} copy-done((bf16[1,128,3072]{2,1,0:T(8,128)(2,1)S(1)}, bf16[1,128,3072]{2,1,0:T(8,128)(2,1)}, u32[]{:S(2)}) %copy-start.2) | copy-done | bytes 786456
  4.7 0.0 copy-start.3
  4.7 1.1 %copy-done.3 = bf16[1,128,3072]{2,1,0:T(8,128)(2,1)S(1)} copy-done((bf16[1,128,3072]{2,1,0:T(8,128)(2,1)S(1)}, bf16[1,128,3072]{2,1,0:T(8,128)(2,1)}, u32[]{:S(2)}) %copy-start.3) | copy-done | bytes 786456
  5.9 0.0 copy-start.4
  5.9 0.9 %copy-done.4 = bf16[48,1536]{1,0:T(8,128)(2,1)S(1)} copy-done((bf16[48,1536]{1,0:T(8,128)(2,1)S(1)}, bf16[48,1536]{1,0:T(8,128)(2,1)}, u32[]{:S(2)}) %copy-start.4) | copy-done | bytes 147480
  6.8 0.0 copy-start.5
  6.8 0.9 %copy-done.5 = bf16[48,1536]{1,0:T(8,128)(2,1)S(1)} copy-done((bf16[48,1536]{1,0:T(8,128)(2,1)S(1)}, bf16[48,1536]{1,0:T(8,128)(2,1)}, u32[]{:S(2)}) %copy-start.5) | copy-done | bytes 147480
  7.7 0.0 copy-start.6
  7.7 0.8 %copy-done.6 = bf16[1,128,128]{2,1,0:T(8,128)(2,1)S(1)} copy-done((bf16[1,128,128]{2,1,0:T(8,128)(2,1)S(1)}, bf16[1,128,128]{2,1,0:T(8,128)(2,1)}, u32[]{:S(2)}) %copy-start.6) | copy-done | bytes 32792
  8.4 28.6 %shard_map.121 = (bf16[48,384]{1,0:T(8,128)(2,1)S(1)}, f32[1,128,128]{2,1,0:T(8,128)S(1)}, f32[1,128,1536]{2,1,0:T(8,128)S(1)}) custom-call(bf16[48,1536]{1,0:T(8,128)(2,1)S(1)} %copy-done.4, bf16[48,1536]{1,0:T(8,128)(2,1)S(1)} %copy-done.5, s32[2,48]{1,0:T(2,128)S(1)} %bitcast.7, bf16[2,48]{1,0:T(2,128)(2,1)S(1)} %bitcast.8, s32[1,48]{1,0:T(1,128)S(1)} %bitcast.9, ...), custom_call_target="tpu_custom_call" | custom-call | flops 1000000000 | bytes 8000000 | tf_op jit(solution)/shard_map/pallas_call | solution.py:418
  37.0 0.6 %copy.16 = bf16[48,384]{1,0:T(8,128)(2,1)} copy(bf16[48,384]{1,0:T(8,128)(2,1)S(1)} %get-tuple-element.6) | data formatting | bytes 73728
  37.6 0.6 %copy.17 = f32[1,128,128]{2,1,0:T(8,128)} copy(f32[1,128,128]{2,1,0:T(8,128)S(1)} %get-tuple-element.7) | data formatting | bytes 131072
  38.3 0.9 %copy.18 = f32[1,128,1536]{2,1,0:T(8,128)} copy(f32[1,128,1536]{2,1,0:T(8,128)S(1)} %get-tuple-element.8) | data formatting | bytes 1572864
Async XLA Ops:
  0.6 0.7 %copy-start.9 = (s32[48]{0:T(128)S(1)}, s32[48]{0:T(128)}, u32[]{:S(2)}) copy-start(s32[48]{0:T(128)} %param.14) | copy-start | bytes 580
  0.6 0.7 %copy-start.7 = (s32[48,2]{0,1:T(2,128)S(1)}, s32[48,2]{0,1:T(2,128)}, u32[]{:S(2)}) copy-start(s32[48,2]{0,1:T(2,128)} %param.12) | copy-start | bytes 1156
  0.7 0.7 %copy-start.8 = (bf16[48,2]{0,1:T(2,128)(2,1)S(1)}, bf16[48,2]{0,1:T(2,128)(2,1)}, u32[]{:S(2)}) copy-start(bf16[48,2]{0,1:T(2,128)(2,1)} %param.13) | copy-start | bytes 580
  1.3 1.1 %copy-start = (bf16[1,3072,128]{2,1,0:T(8,128)(2,1)S(1)}, bf16[1,3072,128]{2,1,0:T(8,128)(2,1)}, u32[]{:S(2)}) copy-start(bf16[1,3072,128]{2,1,0:T(8,128)(2,1)} %param.15) | copy-start | bytes 2359300
  2.5 1.1 %copy-start.1 = (bf16[1,3072,128]{2,1,0:T(8,128)(2,1)S(1)}, bf16[1,3072,128]{2,1,0:T(8,128)(2,1)}, u32[]{:S(2)}) copy-start(bf16[1,3072,128]{2,1,0:T(8,128)(2,1)} %param.16) | copy-start | bytes 2359300
  3.6 1.1 %copy-start.2 = (bf16[1,128,3072]{2,1,0:T(8,128)(2,1)S(1)}, bf16[1,128,3072]{2,1,0:T(8,128)(2,1)}, u32[]{:S(2)}) copy-start(bf16[1,128,3072]{2,1,0:T(8,128)(2,1)} %wd_ref.1) | copy-start | bytes 2359300
  4.7 1.1 %copy-start.3 = (bf16[1,128,3072]{2,1,0:T(8,128)(2,1)S(1)}, bf16[1,128,3072]{2,1,0:T(8,128)(2,1)}, u32[]{:S(2)}) copy-start(bf16[1,128,3072]{2,1,0:T(8,128)(2,1)} %aout_ref.1) | copy-start | bytes 2359300
  5.9 0.9 %copy-start.4 = (bf16[48,1536]{1,0:T(8,128)(2,1)S(1)}, bf16[48,1536]{1,0:T(8,128)(2,1)}, u32[]{:S(2)}) copy-start(bf16[48,1536]{1,0:T(8,128)(2,1)} %tok_ref.1) | copy-start | bytes 442372
  6.8 0.9 %copy-start.5 = (bf16[48,1536]{1,0:T(8,128)(2,1)S(1)}, bf16[48,1536]{1,0:T(8,128)(2,1)}, u32[]{:S(2)}) copy-start(bf16[48,1536]{1,0:T(8,128)(2,1)} %cot_ref.1) | copy-start | bytes 442372
  7.7 0.8 %copy-start.6 = (bf16[1,128,128]{2,1,0:T(8,128)(2,1)S(1)}, bf16[1,128,128]{2,1,0:T(8,128)(2,1)}, u32[]{:S(2)}) copy-start(bf16[1,128,128]{2,1,0:T(8,128)(2,1)} %ain_ref.1) | copy-start | bytes 98308

commit v2 on v1

--- a/solution.py
+++ b/solution.py
@@ -177,15 +177,15 @@
 
 def layer_kernel(
     sizes,
-    tok_ref, cot_ref, ids_ref, prob_ref, ten_ref, wg_ref, wu_ref, wd_ref, ain_ref, aout_ref,
-    dx_ref, ga_ref, gb_ref,
-    rows, send, wgu, wgb, wda, ain, mine, theirs, hid, grads, out_part, in_part, back_send, back, kept, low_mine, low_theirs,
-    local_sem, w_send, w_recv, z_send, z_recv, p_send, p_recv, s_send, s_recv,
+    tok_hbm, cot_hbm, ids_hbm, prob_hbm, ten_hbm, wg_ref, wu_ref, wd_ref, ain_ref, aout_ref,
+    dx_hbm, ga_hbm, gb_hbm,
+    dx_ref, ga_ref, gb_ref, tok_ref, cot_ref, ids_ref, prob_ref, ten_ref, rows, send, wgu, wgb, wda, ain, mine, theirs, hid, grads, out_part, in_part, back_send, back, kept, low_mine, low_theirs,
+    out_sem, in_sem, local_sem, w_send, w_recv, z_send, z_recv, p_send, p_recv, s_send, s_recv,
     r_send, r_recv, b_send, b_recv, l_send, l_recv,
 ):
     dp, ex, tn = sizes
     d, e, t = lax.axis_index("dp"), lax.axis_index("expert"), lax.axis_index("tensor")
-    tokg, half = tok_ref.shape
+    tokg, half = tok_hbm.shape
     wide = half // dp
     ff = wg_ref.shape[3]
     low = ain_ref.shape[2]
@@ -198,6 +198,15 @@
             pl.semaphore_signal(
                 barrier, inc=1, device_id={axis: partner(index, step)}, device_id_type=MESH
             )
+
+    loads = [
+        pltpu.make_async_copy(s, o, in_sem.at[i])
+        for i, (s, o) in enumerate(
+            ((ids_hbm, ids_ref), (prob_hbm, prob_ref), (ten_hbm, ten_ref), (tok_hbm, tok_ref), (cot_hbm, cot_ref))
+        )
+    ]
+    for c in loads:
+        c.start()
 
     def remote(src, dst, ssem, rsem, axis, to):
         return pltpu.make_async_remote_copy(
@@ -231,6 +240,8 @@
     for c in local:
         c.start()
 
+    for c in loads[:3]:
+        c.wait()
     ti = lax.broadcasted_iota(jnp.int32, (tokg, tokg), 0)
     tj = lax.broadcasted_iota(jnp.int32, (tokg, tokg), 1)
 
@@ -255,6 +266,8 @@
     tmark = jnp.where(tcol == lowcol, 1.0, 0.0).astype(BF16)
     marks = tdot((disp * weight).astype(BF16), tmark).astype(BF16)
     disp = disp.astype(BF16)
+    for c in loads[3:]:
+        c.wait()
     mycols = lanes(d * wide, wide)
     sx = tdot(disp, tok_ref[:, mycols]).astype(BF16)
     sy = tdot(disp, cot_ref[:, mycols]).astype(BF16)
@@ -265,11 +278,16 @@
     pl.semaphore_wait(barrier, (tn - 1) + (dp - 1) + (ex - 1))
 
     sends = []
-    for step in range(1, ex):
-        to = partner(e, step)
-        c = remote(send.at[to], rows.at[e, d], z_send.at[step], z_recv.at[e], "expert", to)
-        c.start()
-        sends.append(c)
+    z_parts = (pl.ds(0, wide), pl.ds(wide, wide + low))
+    p_parts = (pl.ds(0, wide), pl.ds(wide, wide))
+    for i, part in enumerate(z_parts):
+        for step in range(1, ex):
+            to = partner(e, step)
+            c = remote(
+                send.at[to, :, part], rows.at[e, d, :, part], z_send.at[step, i], z_recv.at[e, i], "expert", to
+            )
+            c.start()
+            sends.append(c)
     for step in range(1, tn):
         to = partner(t, step)
         for i, (s, o) in enumerate(weight_parts(to, t)):
@@ -288,15 +306,17 @@
         rows[e, k, :, wide:2 * wide] = tdot(disp_own, cot_ref[:, cols]).astype(BF16)
     rows[e, d, :, 2 * wide:] = send[e, :, 2 * wide:]
 
-    for step in range(1, ex):
-        g = partner(e, step)
-        remote(send.at[g], rows.at[g, d], z_send.at[step], z_recv.at[g], "expert", g).wait_recv()
-        for hop in range(1, dp):
-            to = partner(d, hop)
-            part = rows.at[g, d, :, pl.ds(0, 2 * wide)]
-            c = remote(part, part, p_send.at[step, hop], p_recv.at[g, d], "dp", to)
-            c.start()
-            sends.append(c)
+    for i in range(2):
+        for step in range(1, ex):
+            g = partner(e, step)
+            part = rows.at[g, d, :, z_parts[i]]
+            remote(part, part, z_send.at[step, i], z_recv.at[g, i], "expert", g).wait_recv()
+            for hop in range(1, dp):
+                to = partner(d, hop)
+                part = rows.at[g, d, :, p_parts[i]]
+                c = remote(part, part, p_send.at[step, hop, i], p_recv.at[g, d, i], "dp", to)
+                c.start()
+                sends.append(c)
 
     for c in local:
         c.wait()
@@ -325,8 +345,9 @@
         if step:
             for hop in range(1, dp):
                 frm = partner(d, hop)
-                part = rows.at[g, frm, :, pl.ds(0, 2 * wide)]
-                remote(part, part, p_send.at[step, hop], p_recv.at[g, frm], "dp", frm).wait_recv()
+                for i in range(2):
+                    part = rows.at[g, frm, :, p_parts[i]]
+                    remote(part, part, p_send.at[step, hop, i], p_recv.at[g, frm, i], "dp", frm).wait_recv()
         products(g)
 
     for step in range(ex):
@@ -365,13 +386,19 @@
             c.start()
             sends.append(c)
     own = slice_grad(d).reshape(ex, CAP, wide)
-    low_mine[...] = jnp.dot(hidden, a_in, preferred_element_type=F32)
+    low_part = jnp.dot(hidden, a_in, preferred_element_type=F32)
+    low_mine[...] = low_part.astype(BF16)
     for hop in range(1, dp):
         c = remote(low_mine, low_theirs.at[d], l_send.at[hop], l_recv.at[d], "dp", partner(d, hop))
         c.start()
         sends.append(c)
     kept[...] = own
-    ga_ref[0] = tdot(hid[:, lanes(t * ff, ff)], down_coef)
+    ga_ref[...] = tdot(hid[:, lanes(t * ff, ff)], down_coef)
+    results = [
+        pltpu.make_async_copy(s, o, out_sem.at[i])
+        for i, (s, o) in enumerate(((dx_ref, dx_hbm), (ga_ref, ga_hbm.at[0]), (gb_ref, gb_hbm.at[0])))
+    ]
+    results[1].start()
 
     for step in range(ex - 1, -1, -1):
         g = partner(e, step)
@@ -388,22 +415,37 @@
         else:
             back[e] = acc.astype(BF16)
 
-    low_in = low_mine[...]
+    low_in = low_part
     for hop in range(1, dp):
         frm = partner(d, hop)
         remote(low_mine, low_theirs.at[frm], l_send.at[hop], l_recv.at[frm], "dp", frm).wait_recv()
-    low_in = low_in + sum(low_theirs[partner(d, hop)] for hop in range(1, dp))
+    low_in = low_in + sum(low_theirs[partner(d, hop)].astype(F32) for hop in range(1, dp))
     up_coef = (flags * low_in).astype(BF16)
     for k in range(dp):
         y = rows[:, k, :, wide:2 * wide].reshape(slots, wide)
-        gb_ref[0, :, k * wide:(k + 1) * wide] = tdot(up_coef, y)
+        gb_ref[:, k * wide:(k + 1) * wide] = tdot(up_coef, y)
+    results[2].start()
 
     for step in range(1, ex):
         g = partner(e, step)
         remote(back_send.at[step], back.at[g], b_send.at[step], b_recv.at[g], "expert", g).wait_recv()
     dx_ref[...] = jnp.dot(disp, back[...].reshape(slots, wide), preferred_element_type=F32).astype(BF16)
+    results[0].start()
     for c in sends:
         c.wait_send()
+    for c in results:
+        c.wait()
+
+
+def write_kernel(a_ref, b_ref, c_ref, a_out, b_out, c_out, sem):
+    copies = [
+        pltpu.make_async_copy(s, o, sem.at[i])
+        for i, (s, o) in enumerate(((c_ref, c_out), (b_ref, b_out), (a_ref, a_out)))
+    ]
+    for c in copies:
+        c.start()
+    for c in copies:
+        c.wait()
 
 
 def fused(sizes, tokens, cotangent, expert_ids, gate_probs, tenant_ids, w_gate, w_up, w_down, adapter_in, adapter_out):
@@ -413,18 +455,27 @@
     ff = w_gate.shape[2]
     low = adapter_in.shape[2]
     hall, slots = tn * ff, ex * CAP
-    vmem, hbm = pl.BlockSpec(memory_space=pltpu.VMEM), pl.BlockSpec(memory_space=pl.ANY)
+    hbm = pl.BlockSpec(memory_space=pltpu.HBM)
     dma = pltpu.SemaphoreType.DMA
-    return pl.pallas_call(
+    shapes = (
+        jax.ShapeDtypeStruct((tokg, wide), BF16),
+        jax.ShapeDtypeStruct((1, ff, low), F32),
+        jax.ShapeDtypeStruct((1, low, half), F32),
+    )
+    results = pl.pallas_call(
         functools.partial(layer_kernel, sizes),
-        out_shape=(
-            jax.ShapeDtypeStruct((tokg, wide), BF16),
-            jax.ShapeDtypeStruct((1, ff, low), F32),
-            jax.ShapeDtypeStruct((1, low, half), F32),
-        ),
-        in_specs=[vmem] * 5 + [hbm] * 5,
-        out_specs=(vmem, vmem, vmem),
+        out_shape=shapes,
+        in_specs=[hbm] * 10,
+        out_specs=(hbm, hbm, hbm),
         scratch_shapes=[
+            pltpu.VMEM((tokg, wide), BF16),
+            pltpu.VMEM((ff, low), F32),
+            pltpu.VMEM((low, half), F32),
+            pltpu.VMEM((tokg, half), BF16),
+            pltpu.VMEM((tokg, half), BF16),
+            pltpu.VMEM((TOP, tokg), jnp.int32),
+            pltpu.VMEM((TOP, tokg), BF16),
+            pltpu.VMEM((1, tokg), jnp.int32),
             pltpu.VMEM((ex, dp, CAP, 2 * wide + low), BF16),
             pltpu.VMEM((ex, CAP, 2 * wide + low), BF16),
             pltpu.VMEM((dp // tn, tn, wide, 2 * hall), BF16),
@@ -440,22 +491,31 @@
             pltpu.VMEM((ex, CAP, wide), BF16),
             pltpu.VMEM((ex, CAP, wide), BF16),
             pltpu.VMEM((ex, CAP, wide), F32),
-            pltpu.VMEM((slots, low), F32),
-            pltpu.VMEM((dp, slots, low), F32),
+            pltpu.VMEM((slots, low), BF16),
+            pltpu.VMEM((dp, slots, low), BF16),
+            dma((3,)), dma((5,)),
             dma((7,)),
             dma((tn, 6)), dma((tn, 6)),
-            dma((ex,)), dma((ex,)),
-            dma((ex, dp)), dma((ex, dp)),
+            dma((ex, 2)), dma((ex, 2)),
+            dma((ex, dp, 2)), dma((ex, dp, 2)),
             dma((tn, ex)), dma((tn, ex)),
             dma((dp, ex)), dma((dp, ex)),
             dma((ex,)), dma((ex,)),
             dma((dp,)), dma((dp,)),
         ],
         compiler_params=pltpu.CompilerParams(
-            collective_id=0, has_side_effects=True, vmem_limit_bytes=40 * 1024 * 1024
+            collective_id=0, has_side_effects=True, vmem_limit_bytes=62 * 1024 * 1024
         ),
         cost_estimate=pl.CostEstimate(flops=10**9, bytes_accessed=8 * 10**6, transcendentals=10**5),
     )(tokens, cotangent, expert_ids.T, gate_probs.T, tenant_ids.reshape(1, -1), w_gate.reshape(dp, tn, wide, ff), w_up.reshape(dp, tn, wide, ff), w_down, adapter_in, adapter_out)
+    return pl.pallas_call(
+        write_kernel,
+        out_shape=shapes,
+        in_specs=[hbm] * 3,
+        out_specs=(hbm,) * 3,
+        scratch_shapes=[dma((3,))],
+        compiler_params=pltpu.CompilerParams(vmem_limit_bytes=62 * 1024 * 1024),
+    )(*results)
 
 
 def body_for(mesh):

time: 39.6 us -> 59.3 us (1.50)
  Pallas kernels: 28.6 us -> 58.5 us
  local copies, waits for them, and re-layouts: 9.91 us -> 0 us
    pallas_call x1 -> x2, Pallas kernels: 28.6 us -> 58.5 us  [the longest x1 30.5 us: fused(): pl.pallas_call(functools.partial(layer_kernel, sizes), out_shape=shapes,...]
    unnamed x23 -> x0, local copies, waits for them, and re-layouts: 9.91 us -> none
where the time goes in v2:
time: 59.3 us; the launch traced here: 59.2 us
  Pallas kernels  58.5 us (99%)
  between operations  0.64 us (1%)
    pallas_call x1, Pallas kernels, fused(): pl.pallas_call(functools.partial(layer_kernel, sizes), out_shape=shapes,...  30.5 us
    pallas_call x1, Pallas kernels, fused(): pl.pallas_call(write_kernel, out_shape=shapes, in_specs=[hbm] * 3, out_sp...  28.1 us

profile of v2, /device:TPU:0, one launch (start us, length us, event | category | flops | bytes accessed | tf_op | source)
XLA Modules:
  0.0 59.2 jit_solution(2408815722500197258)
XLA Ops:
  0.6 30.5 %shard_map.121 = (bf16[48,384]{1,0:T(8,128)(2,1)}, f32[1,128,128]{2,1,0:T(8,128)}, f32[1,128,1536]{2,1,0:T(8,128)}) custom-call(bf16[48,1536]{1,0:T(8,128)(2,1)} %tok_hbm.1, bf16[48,1536]{1,0:T(8,128)(2,1)} %cot_hbm.1, s32[2,48]{1,0:T(2,128)} %bitcast.7, bf16[2,48]{1,0:T(2,128)(2,1)} %bitcast.8, s32[1,48]{1,0:T(1,128)} %bitcast.9, ...), custom_call_target="tpu_custom_call" | custom-call | flops 1000000000 | bytes 8000000 | tf_op jit(solution)/shard_map/pallas_call | solution.py:465
  31.1 28.1 %shard_map.122 = (bf16[48,384]{1,0:T(8,128)(2,1)}, f32[1,128,128]{2,1,0:T(8,128)}, f32[1,128,1536]{2,1,0:T(8,128)}) custom-call(bf16[48,384]{1,0:T(8,128)(2,1)} %get-tuple-element.6.a_ref, f32[1,128,128]{2,1,0:T(8,128)} %get-tuple-element.7.b_ref, f32[1,128,1536]{2,1,0:T(8,128)} %get-tuple-element.8.c_ref), custom_call_target="tpu_custom_call" | custom-call | tf_op jit(solution)/shard_map/pallas_call | solution.py:511

commit v3 on v2

--- a/solution.py
+++ b/solution.py
@@ -179,7 +179,7 @@
     sizes,
     tok_hbm, cot_hbm, ids_hbm, prob_hbm, ten_hbm, wg_ref, wu_ref, wd_ref, ain_ref, aout_ref,
     dx_hbm, ga_hbm, gb_hbm,
-    dx_ref, ga_ref, gb_ref, tok_ref, cot_ref, ids_ref, prob_ref, ten_ref, rows, send, wgu, wgb, wda, ain, mine, theirs, hid, grads, out_part, in_part, back_send, back, kept, low_mine, low_theirs,
+    dx_ref, ga_ref, gb_ref, tok_ref, cot_ref, ids_ref, prob_ref, ten_ref, rows, send, wgu, wgb, wda, ain, gu_mine, gu_theirs, bl_mine, bl_theirs, silu_keep, slope_keep, hid, grads, out_part, in_part, back_send, back, kept, low_mine, low_theirs,
     out_sem, in_sem, local_sem, w_send, w_recv, z_send, z_recv, p_send, p_recv, s_send, s_recv,
     r_send, r_recv, b_send, b_recv, l_send, l_recv,
 ):
@@ -260,40 +260,50 @@
     before = jnp.where(ti > tj, 1.0, 0.0).astype(BF16)
     place = jnp.dot(before, named.astype(BF16), preferred_element_type=F32)
     disp = jnp.where(place == scol.astype(F32), named, 0.0)
+    disp = disp.astype(BF16)
+    for c in loads[3:]:
+        c.wait()
+    mycols = lanes(d * wide, wide)
+    send[:, :, 0:wide] = tdot(disp, tok_ref[:, mycols]).astype(BF16).reshape(ex, CAP, wide)
+
+    pl.semaphore_wait(barrier, (tn - 1) + (dp - 1) + (ex - 1))
+
+    sends = []
+    z_parts = (pl.ds(0, wide), pl.ds(wide, wide + low))
+    p_parts = (pl.ds(0, wide), pl.ds(wide, wide))
+
+    def dispatch(i):
+        for step in range(1, ex):
+            to = partner(e, step)
+            c = remote(
+                send.at[to, :, z_parts[i]], rows.at[e, d, :, z_parts[i]],
+                z_send.at[step, i], z_recv.at[e, i], "expert", to,
+            )
+            c.start()
+            sends.append(c)
+
+    dispatch(0)
+    send[:, :, wide:2 * wide] = tdot(disp, cot_ref[:, mycols]).astype(BF16).reshape(ex, CAP, wide)
     weight = jnp.where(hit0, prob0, 0.0) + jnp.where(hit1, prob1, 0.0)
     tcol = column(ten_ref[...])
     lowcol = lax.div(lax.broadcasted_iota(jnp.int32, (tokg, low), 1), RANK).astype(F32)
     tmark = jnp.where(tcol == lowcol, 1.0, 0.0).astype(BF16)
-    marks = tdot((disp * weight).astype(BF16), tmark).astype(BF16)
-    disp = disp.astype(BF16)
-    for c in loads[3:]:
-        c.wait()
-    mycols = lanes(d * wide, wide)
-    sx = tdot(disp, tok_ref[:, mycols]).astype(BF16)
-    sy = tdot(disp, cot_ref[:, mycols]).astype(BF16)
-    send[:, :, 0:wide] = sx.reshape(ex, CAP, wide)
-    send[:, :, wide:2 * wide] = sy.reshape(ex, CAP, wide)
-    send[:, :, 2 * wide:] = marks.reshape(ex, CAP, low)
-
-    pl.semaphore_wait(barrier, (tn - 1) + (dp - 1) + (ex - 1))
-
-    sends = []
-    z_parts = (pl.ds(0, wide), pl.ds(wide, wide + low))
-    p_parts = (pl.ds(0, wide), pl.ds(wide, wide))
-    for i, part in enumerate(z_parts):
-        for step in range(1, ex):
-            to = partner(e, step)
-            c = remote(
-                send.at[to, :, part], rows.at[e, d, :, part], z_send.at[step, i], z_recv.at[e, i], "expert", to
-            )
-            c.start()
-            sends.append(c)
+    marked = jnp.where(disp > 0, weight, 0.0).astype(BF16)
+    send[:, :, 2 * wide:] = tdot(marked, tmark).astype(BF16).reshape(ex, CAP, low)
+    dispatch(1)
     for step in range(1, tn):
         to = partner(t, step)
         for i, (s, o) in enumerate(weight_parts(to, t)):
             c = remote(s, o, w_send.at[step, i], w_recv.at[t, i], "tensor", to)
             c.start()
             sends.append(c)
+
+    def weights_here(i):
+        local[i].wait()
+        for step in range(1, tn):
+            frm = partner(t, step)
+            s, o = weight_parts(t, frm)[i]
+            remote(s, o, w_send.at[step, i], w_recv.at[frm, i], "tensor", frm).wait_recv()
 
     scol_own = lax.broadcasted_iota(jnp.int32, (tokg, CAP), 1).astype(F32)
     named_own = jnp.where((ids0 == e) | (ids1 == e), 1.0, 0.0)
@@ -306,73 +316,84 @@
         rows[e, k, :, wide:2 * wide] = tdot(disp_own, cot_ref[:, cols]).astype(BF16)
     rows[e, d, :, 2 * wide:] = send[e, :, 2 * wide:]
 
-    for i in range(2):
+    def pass_on(i):
         for step in range(1, ex):
             g = partner(e, step)
             part = rows.at[g, d, :, z_parts[i]]
             remote(part, part, z_send.at[step, i], z_recv.at[g, i], "expert", g).wait_recv()
             for hop in range(1, dp):
-                to = partner(d, hop)
                 part = rows.at[g, d, :, p_parts[i]]
-                c = remote(part, part, p_send.at[step, hop, i], p_recv.at[g, d, i], "dp", to)
+                c = remote(part, part, p_send.at[step, hop, i], p_recv.at[g, d, i], "dp", partner(d, hop))
                 c.start()
                 sends.append(c)
 
-    for c in local:
-        c.wait()
-    for step in range(1, tn):
-        frm = partner(t, step)
-        for i, (s, o) in enumerate(weight_parts(t, frm)):
-            remote(s, o, w_send.at[step, i], w_recv.at[frm, i], "tensor", frm).wait_recv()
-
-    def products(g):
-        gu = jnp.zeros((CAP, 2 * hall), F32)
-        bl = jnp.zeros((CAP, hall + low), F32)
-        for k in range(dp):
-            f = slice(k * wide, (k + 1) * wide)
-            gu = gu + jnp.dot(rows[g, k, :, 0:wide], wgu[k // tn, k % tn], preferred_element_type=F32)
-            bl = bl + ndot(rows[g, k, :, wide:2 * wide], wda[:, f])
-        mine[g, :, 0:2 * hall] = gu
-        mine[g, :, 2 * hall:] = bl
-        for hop in range(1, tn):
-            to = partner(t, hop)
-            c = remote(mine.at[g], theirs.at[t, g], s_send.at[hop, step], s_recv.at[t, g], "tensor", to)
+    def gathered(i, hop):
+        frm = partner(d, hop)
+        if hop:
+            for step in range(1, ex):
+                g = partner(e, step)
+                part = rows.at[g, frm, :, p_parts[i]]
+                remote(part, part, p_send.at[step, hop, i], p_recv.at[g, frm, i], "dp", frm).wait_recv()
+        return frm, rows[:, frm, :, i * wide:(i + 1) * wide].reshape(slots, wide)
+
+    def exchange(i, acc, own, others):
+        own[...] = acc
+        copies = [
+            remote(own, others.at[t], s_send.at[hop, i], s_recv.at[t, i], "tensor", partner(t, hop))
+            for hop in range(1, tn)
+        ]
+        for c in copies:
             c.start()
-            sends.append(c)
-
-    for step in range(ex):
-        g = partner(e, step)
-        if step:
-            for hop in range(1, dp):
-                frm = partner(d, hop)
-                for i in range(2):
-                    part = rows.at[g, frm, :, p_parts[i]]
-                    remote(part, part, p_send.at[step, hop, i], p_recv.at[g, frm, i], "dp", frm).wait_recv()
-        products(g)
-
-    for step in range(ex):
-        g = partner(e, step)
+        sends.extend(copies)
+
+    def exchanged(i, own, others):
+        total = own[...]
         for hop in range(1, tn):
             frm = partner(t, hop)
-            remote(mine.at[g], theirs.at[frm, g], s_send.at[hop, step], s_recv.at[frm, g], "tensor", frm).wait_recv()
-    total = mine[...].reshape(slots, -1)
-    for hop in range(1, tn):
-        total = total + theirs[partner(t, hop)].reshape(slots, -1)
-    gate, up = total[:, 0:hall], total[:, hall:2 * hall]
-    back_acc, low_acc = total[:, 2 * hall:3 * hall], total[:, 3 * hall:]
+            remote(own, others.at[frm], s_send.at[hop, i], s_recv.at[frm, i], "tensor", frm).wait_recv()
+            total = total + others[frm]
+        return total
+
+    pass_on(0)
+    weights_here(0)
+    weights_here(1)
+    acc = jnp.zeros((slots, 2 * hall), F32)
+    for hop in range(dp):
+        k, x = gathered(0, hop)
+        acc = acc + jnp.dot(x, wgu[lax.div(k, tn), lax.rem(k, tn)], preferred_element_type=F32)
+    exchange(0, acc, gu_mine, gu_theirs)
+    pass_on(1)
+    weights_here(2)
+    weights_here(3)
+    local[6].wait()
     flags = rows[:, d, :, 2 * wide:].reshape(slots, low).astype(F32)
     row_weight = jnp.max(flags, axis=1, keepdims=True)
     flags = adapter_scale_factor * flags
+    total = exchanged(0, gu_mine, gu_theirs)
+    gate, up = total[:, 0:hall], total[:, hall:]
     sig = jax.nn.sigmoid(gate)
     silu = gate * sig
     hidden = (silu * up).astype(BF16)
     hid[...] = hidden
+    a_in = ain[...]
+    low_part = jnp.dot(hidden, a_in, preferred_element_type=F32)
+    low_mine[...] = low_part.astype(BF16)
+    silu_keep[...] = silu
+    slope_keep[...] = up * (sig * (1.0 + gate * (1.0 - sig)))
+
+    acc = jnp.zeros((slots, hall + low), F32)
+    for hop in range(dp):
+        k, y = gathered(1, hop)
+        acc = acc + ndot(y, wda[:, lanes(k * wide, wide)])
+    exchange(1, acc, bl_mine, bl_theirs)
+    weights_here(4)
+    weights_here(5)
+    total = exchanged(1, bl_mine, bl_theirs)
+    back_acc, low_acc = total[:, 0:hall], total[:, hall:]
     down_coef = (flags * low_acc).astype(BF16)
-    a_in = ain[...]
     hidden_grad = row_weight * back_acc + ndot(down_coef, a_in)
-    slope = sig * (1.0 + gate * (1.0 - sig))
-    grads[:, 0:hall] = (hidden_grad * up * slope).astype(BF16)
-    grads[:, hall:] = (hidden_grad * silu).astype(BF16)
+    grads[:, 0:hall] = (hidden_grad * slope_keep[...]).astype(BF16)
+    grads[:, hall:] = (hidden_grad * silu_keep[...]).astype(BF16)
 
     def slice_grad(k):
         return ndot(grads[...], wgb[k])
@@ -386,8 +407,6 @@
             c.start()
             sends.append(c)
     own = slice_grad(d).reshape(ex, CAP, wide)
-    low_part = jnp.dot(hidden, a_in, preferred_element_type=F32)
-    low_mine[...] = low_part.astype(BF16)
     for hop in range(1, dp):
         c = remote(low_mine, low_theirs.at[d], l_send.at[hop], l_recv.at[d], "dp", partner(d, hop))
         c.start()
@@ -437,14 +456,23 @@
         c.wait()
 
 
-def write_kernel(a_ref, b_ref, c_ref, a_out, b_out, c_out, sem):
-    copies = [
-        pltpu.make_async_copy(s, o, sem.at[i])
-        for i, (s, o) in enumerate(((c_ref, c_out), (b_ref, b_out), (a_ref, a_out)))
-    ]
-    for c in copies:
+def write_kernel(a_ref, b_ref, c_ref, a_out, b_out, c_out, a_mid, b_mid, c_mid, in_sem, out_sem):
+    halves = c_ref.shape[1] // 2
+    first, second = pl.ds(0, halves), pl.ds(halves, halves)
+    routes = (
+        (c_ref.at[:, first], c_mid.at[:, first], c_out.at[:, first]),
+        (c_ref.at[:, second], c_mid.at[:, second], c_out.at[:, second]),
+        (b_ref, b_mid, b_out),
+        (a_ref, a_mid, a_out),
+    )
+    loads = [pltpu.make_async_copy(s, m, in_sem.at[i]) for i, (s, m, _) in enumerate(routes)]
+    stores = [pltpu.make_async_copy(m, o, out_sem.at[i]) for i, (_, m, o) in enumerate(routes)]
+    for c in loads:
         c.start()
-    for c in copies:
+    for load, store in zip(loads, stores):
+        load.wait()
+        store.start()
+    for c in stores:
         c.wait()
 
 
@@ -482,8 +510,12 @@
             pltpu.VMEM((dp, wide, 2 * hall), BF16),
             pltpu.VMEM((hall + low, half), BF16),
             pltpu.VMEM((hall, low), BF16),
-            pltpu.VMEM((ex, CAP, 3 * hall + low), F32),
-            pltpu.VMEM((tn, ex, CAP, 3 * hall + low), F32),
+            pltpu.VMEM((slots, 2 * hall), F32),
+            pltpu.VMEM((tn, slots, 2 * hall), F32),
+            pltpu.VMEM((slots, hall + low), F32),
+            pltpu.VMEM((tn, slots, hall + low), F32),
+            pltpu.VMEM((slots, hall), F32),
+            pltpu.VMEM((slots, hall), F32),
             pltpu.VMEM((slots, hall), BF16),
             pltpu.VMEM((slots, 2 * hall), BF16),
             pltpu.VMEM((dp, ex, CAP, wide), BF16),
@@ -498,7 +530,7 @@
             dma((tn, 6)), dma((tn, 6)),
             dma((ex, 2)), dma((ex, 2)),
             dma((ex, dp, 2)), dma((ex, dp, 2)),
-            dma((tn, ex)), dma((tn, ex)),
+            dma((tn, 2)), dma((tn, 2)),
             dma((dp, ex)), dma((dp, ex)),
             dma((ex,)), dma((ex,)),
             dma((dp,)), dma((dp,)),
@@ -513,7 +545,7 @@
         out_shape=shapes,
         in_specs=[hbm] * 3,
         out_specs=(hbm,) * 3,
-        scratch_shapes=[dma((3,))],
+        scratch_shapes=[pltpu.VMEM(r.shape, r.dtype) for r in results] + [dma((4,)), dma((4,))],
         compiler_params=pltpu.CompilerParams(vmem_limit_bytes=62 * 1024 * 1024),
     )(*results)
 

time: 59.3 us -> 34.5 us (0.58)
  the two profiles are of different devices: /device:TPU:0 before, /device:TPU:1 now
where the time goes in v3:
time: 34.5 us; the launch traced here: 34.4 us
  Pallas kernels  33.7 us (98%)
  between operations  0.64 us (2%)
    pallas_call x1, Pallas kernels, fused(): pl.pallas_call(functools.partial(layer_kernel, sizes), out_shape=shapes,...  31.8 us
    pallas_call x1, Pallas kernels, fused(): pl.pallas_call(write_kernel, out_shape=shapes, in_specs=[hbm] * 3, out_sp...  1.96 us

profile of v3, /device:TPU:1, one launch (start us, length us, event | category | flops | bytes accessed | tf_op | source)
XLA Modules:
  0.0 34.4 jit_solution(7864020905126582837)
XLA Ops:
  0.6 31.8 %shard_map.121 = (bf16[48,384]{1,0:T(8,128)(2,1)}, f32[1,128,128]{2,1,0:T(8,128)}, f32[1,128,1536]{2,1,0:T(8,128)}) custom-call(bf16[48,1536]{1,0:T(8,128)(2,1)} %tok_hbm.1, bf16[48,1536]{1,0:T(8,128)(2,1)} %cot_hbm.1, s32[2,48]{1,0:T(2,128)} %bitcast.7, bf16[2,48]{1,0:T(2,128)(2,1)} %bitcast.8, s32[1,48]{1,0:T(1,128)} %bitcast.9, ...), custom_call_target="tpu_custom_call" | custom-call | flops 1000000000 | bytes 8000000 | tf_op jit(solution)/shard_map/pallas_call | solution.py:493
  32.4 2.0 %shard_map.122 = (bf16[48,384]{1,0:T(8,128)(2,1)}, f32[1,128,128]{2,1,0:T(8,128)}, f32[1,128,1536]{2,1,0:T(8,128)}) custom-call(bf16[48,384]{1,0:T(8,128)(2,1)} %get-tuple-element.6.a_ref, f32[1,128,128]{2,1,0:T(8,128)} %get-tuple-element.7.b_ref, f32[1,128,1536]{2,1,0:T(8,128)} %get-tuple-element.8.c_ref), custom_call_target="tpu_custom_call" | custom-call | tf_op jit(solution)/shard_map/pallas_call | solution.py:543

commit v4 on v3

--- a/solution.py
+++ b/solution.py
@@ -355,6 +355,7 @@
         return total
 
     pass_on(0)
+    pass_on(1)
     weights_here(0)
     weights_here(1)
     acc = jnp.zeros((slots, 2 * hall), F32)
@@ -362,7 +363,6 @@
         k, x = gathered(0, hop)
         acc = acc + jnp.dot(x, wgu[lax.div(k, tn), lax.rem(k, tn)], preferred_element_type=F32)
     exchange(0, acc, gu_mine, gu_theirs)
-    pass_on(1)
     weights_here(2)
     weights_here(3)
     local[6].wait()

time: 34.5 us -> 33 us (0.957)
  the two profiles are of different devices: /device:TPU:1 before, /device:TPU:0 now
where the time goes in v4:
time: 33 us; the launch traced here: 32.9 us
  Pallas kernels  32.2 us (98%)
  between operations  0.64 us (2%)
    pallas_call x1, Pallas kernels, fused(): pl.pallas_call(functools.partial(layer_kernel, sizes), out_shape=shapes,...  30.3 us
    pallas_call x1, Pallas kernels, fused(): pl.pallas_call(write_kernel, out_shape=shapes, in_specs=[hbm] * 3, out_sp...  1.96 us

profile of v4, /device:TPU:0, one launch (start us, length us, event | category | flops | bytes accessed | tf_op | source)
XLA Modules:
  0.0 32.9 jit_solution(7949837105684204864)
XLA Ops:
  0.6 30.3 %shard_map.121 = (bf16[48,384]{1,0:T(8,128)(2,1)}, f32[1,128,128]{2,1,0:T(8,128)}, f32[1,128,1536]{2,1,0:T(8,128)}) custom-call(bf16[48,1536]{1,0:T(8,128)(2,1)} %tok_hbm.1, bf16[48,1536]{1,0:T(8,128)(2,1)} %cot_hbm.1, s32[2,48]{1,0:T(2,128)} %bitcast.7, bf16[2,48]{1,0:T(2,128)(2,1)} %bitcast.8, s32[1,48]{1,0:T(1,128)} %bitcast.9, ...), custom_call_target="tpu_custom_call" | custom-call | flops 1000000000 | bytes 8000000 | tf_op jit(solution)/shard_map/pallas_call | solution.py:493
  30.9 2.0 %shard_map.122 = (bf16[48,384]{1,0:T(8,128)(2,1)}, f32[1,128,128]{2,1,0:T(8,128)}, f32[1,128,1536]{2,1,0:T(8,128)}) custom-call(bf16[48,384]{1,0:T(8,128)(2,1)} %get-tuple-element.6.a_ref, f32[1,128,128]{2,1,0:T(8,128)} %get-tuple-element.7.b_ref, f32[1,128,1536]{2,1,0:T(8,128)} %get-tuple-element.8.c_ref), custom_call_target="tpu_custom_call" | custom-call | tf_op jit(solution)/shard_map/pallas_call | solution.py:543
